TPU v7x, 32 devices: a whole 2x2x4 slice. The times are simulated.
32 devices in a mesh: vocab: 8 (over z, y), section: 4 (over x, core).
Axes of the slice: x: 2, y: 2, z: 4, core: 2. Of those that a mesh axis runs over, the one named last changes fastest.
Arguments:
- hidden: bfloat16 [4, 32, 8192], P('section', 'vocab'), may hold values from -64 to 64
- policy_head: bfloat16 [9504, 8192], P(('vocab', 'section')), may hold values from -1 to 1
- reference_head: bfloat16 [9504, 8192], P(('vocab', 'section')), may hold values from -1 to 1
- targets: int32 [4, 32], replicated, may hold values from 0 to 9503
- loss_mask: int32 [4, 32], replicated, may hold values 0 or 1
Outputs:
- token_logprob: float32 [4, 32], replicated
- token_kl: float32 [4, 32], replicated
- totals: float32 [3], replicated
All inputs are finite; a program needn't handle non-finite values.
Results may differ from a plain program's by a relative error of at most 0.0003.
Values may be sent and summed in bfloat16 or wider, within the bound.
A program may use at most 128 MiB of HBM per device.

v0:
```python
import jax
import jax.numpy as jnp
from jax import lax
from jax.sharding import PartitionSpec as P


def shard_moments(hidden_rows, wanted, policy_head, reference_head, offset):
    contract_dims = (((1,), (1,)), ((), ()))
    policy_logits = lax.dot_general(
        hidden_rows, policy_head, contract_dims, preferred_element_type=jnp.float32
    )
    refer_logits = lax.dot_general(
        hidden_rows, reference_head, contract_dims, preferred_element_type=jnp.float32
    )
    policy_top = jnp.max(policy_logits, axis=1)
    policy_shift = policy_logits - policy_top[:, None]
    policy_exp = jnp.exp(policy_shift)
    policy_sum = jnp.sum(policy_exp, axis=1)
    policy_first = jnp.sum(policy_exp * policy_shift, axis=1)
    policy_cross = jnp.sum(policy_exp * (policy_logits - refer_logits), axis=1)
    columns = offset + lax.broadcasted_iota(jnp.int32, (1, policy_head.shape[0]), 1)
    chosen = jnp.sum(jnp.where(wanted[:, None] == columns, policy_logits, 0.0), axis=1)
    refer_top = jnp.max(refer_logits, axis=1)
    refer_sum = jnp.sum(jnp.exp(refer_logits - refer_top[:, None]), axis=1)
    return (policy_top, policy_sum, policy_first, policy_cross, chosen, refer_top, refer_sum)


def place_moments(moments, shape):
    return tuple((moment.reshape(shape) for moment in moments))


def on_device(hidden, policy_head, reference_head, targets, loss_mask):
    width = hidden.shape[2]
    offset = lax.axis_index(("vocab", "section")) * policy_head.shape[0]
    micro_total, token_total = targets.shape
    gathered = lax.all_gather(hidden, "section", axis=0, tiled=True)
    portion = lax.all_gather(gathered, "vocab", axis=1, tiled=True)
    span = portion.shape[1]
    wanted = targets.reshape(-1)
    moments = shard_moments(portion.reshape(-1, width), wanted, policy_head, reference_head, offset)
    moments = place_moments(moments, (micro_total, span))
    local_top, local_sum, local_first, local_cross, local_chosen, local_rtop, local_rsum = moments
    policy_top, refer_top = lax.pmax((local_top, local_rtop), ("vocab", "section"))
    policy_scale = jnp.exp(local_top - policy_top)
    refer_scale = jnp.exp(local_rtop - refer_top)
    policy_sum, policy_first, policy_cross, chosen, refer_sum = lax.psum(
        (
            policy_scale * local_sum,
            policy_scale * (local_first + (local_top - policy_top) * local_sum),
            policy_scale * local_cross,
            local_chosen,
            refer_scale * local_rsum,
        ),
        ("vocab", "section"),
    )
    policy_lse = policy_top + jnp.log(policy_sum)
    refer_lse = refer_top + jnp.log(refer_sum)
    logprob = chosen - policy_lse
    entropy = jnp.log(policy_sum) - policy_first / policy_sum
    divergence = policy_cross / policy_sum - policy_lse + refer_lse
    weights = loss_mask.astype(jnp.float32)
    scale = 1.0 / (micro_total * token_total)
    totals = (
        jnp.stack(
            [jnp.sum(weights * logprob), jnp.sum(weights * entropy), jnp.sum(weights * divergence)]
        )
        * scale
    )
    return (logprob, divergence, totals)


def solution(mesh):
    placed = (
        P("section", "vocab", None),
        P(("vocab", "section"), None),
        P(("vocab", "section"), None),
        P(),
        P(),
    )
    return jax.shard_map(
        on_device, mesh=mesh, in_specs=placed, out_specs=(P(), P(), P()), check_vma=False
    )
```

profile of v0, /device:TPU:0, one launch (start us, length us, event | category | flops | bytes accessed | tf_op | source)
XLA Modules:
  0.0 165.2 jit_solution(4980686287815334519)
XLA Ops:
  7.2 0.0 all-gather.2.cloned.1.call-start
  7.2 7.4 %all_gather.6 = bf16[4,4,8192]{2,1,0:T(4,128)(2,1)S(1)} all-gather(bf16[1,4,8192]{2,1,0:T(4,128)(2,1)} %param.5), channel_id=1, replica_groups=mesh['vocab'=8,'section'=4] {'section'}, dimensions={0}, use_global_device_ids=true | all-gather | bytes 327680 | tf_op jit(solution)/shard_map/all_gather | solution.py:36
  14.6 0.9 copy.9
  15.5 0.0 all-gather.2.cloned.1.call-update
  15.6 0.8 eq.15
  16.3 50.0 %all-gather.2.cloned.1.call-done = bf16[4,32,8192]{2,0,1:T(4,128)(2,1)} async-done(((bf16[4,4,8192]{2,0,1:T(4,128)(2,1)}), bf16[4,32,8192]{2,0,1:T(4,128)(2,1)}) %all-gather.2.cloned.1.call-update) | async-done | bytes 2097168 | tf_op jit(solution)/shard_map/all_gather | solution.py:37
  66.3 0.0 copy-start
  66.3 2.9 %copy.10 = bf16[4,32,8192]{2,1,0:T(8,128)(2,1)S(1)} copy(bf16[4,32,8192]{2,0,1:T(4,128)(2,1)} %all-gather.2.cloned.1.call-done) | data formatting | bytes 4194304 | tf_op jit(solution)/shard_map/all_gather | solution.py:37
  69.2 3.9 %fusion.4 = (f32[128]{0:T(128)S(1)}, f32[128,297]{0,1:T(8,128)S(1)}) fusion(bf16[128,8192]{1,0:T(8,128)(2,1)S(1)} %bitcast.8, bf16[297,8192]{1,0:T(8,128)(2,1)} %param.6), kind=kOutput, calls=%fused_computation.19 | convolution fusion | flops 622892032 | bytes 7115776 | tf_op jit(solution)/shard_map/dot_general | solution.py:9
  73.1 0.0 copy-done
  73.1 0.0 copy-start.1
  73.1 1.5 fusion.5
  74.6 0.1 reshape.40
  74.7 0.1 reshape.43
  74.8 0.1 fusion.1
  74.9 0.1 reshape.41
  75.0 0.1 reshape.42
  75.1 0.1 reshape.44
  75.1 0.1 reshape.45
  75.2 0.1 reshape.39
  75.3 39.2 %all-reduce.1 = (f32[4,32]{1,0:T(4,128)S(1)}, f32[4,32]{1,0:T(4,128)S(1)}) all-reduce(f32[4,32]{1,0:T(4,128)S(1)} %reshape.40, f32[4,32]{1,0:T(4,128)S(1)} %reshape.43), channel_id=1, replica_groups=mesh['vocab'=8,'section'=4] {'vocab','section'}, use_global_device_ids=true, to_apply=%region_3.0 | all-reduce | flops 256 | bytes 2048 | tf_op jit(solution)/shard_map/pmax | solution.py:43
  114.5 40.1 %all-reduce = (f32[4,32]{1,0:T(4,128)S(1)}, f32[4,32]{1,0:T(4,128)S(1)}, f32[4,32]{1,0:T(4,128)S(1)}, f32[4,32]{1,0:T(4,128)S(1)}, f32[4,32]{1,0:T(4,128)S(1)}) all-reduce(f32[4,32]{1,0:T(4,128)S(1)} %reshape.39, f32[4,32]{1,0:T(4,128)S(1)} %get-tuple-element.21, ...), channel_id=1, replica_groups=mesh['vocab'=8,'section'=4] {'vocab','section'}, use_global_device_ids=true, to_apply=%region_1.0 | all-reduce | flops 640 | bytes 5120 | tf_op jit(solution)/shard_map/psum | solution.py:46
  154.6 0.0 copy-done.1
  154.6 1.3 multiply_reduce_fusion.2
  155.9 2.5 %maximum_multiply_fusion = f32[3]{0:T(128)} fusion(f32[1]{0:T(128)} %bitcast.3, f32[1]{0:T(128)} %bitcast.2, f32[1]{0:T(128)} %bitcast.1), kind=kLoop, calls=%fused_computation.18 | loop fusion | flops 9 | bytes 24 | tf_op jit(solution)/shard_map/mul | solution.py:64
  (2 shorter events, 0.0 us)
Async XLA Ops:
  7.2 59.2 %all-gather.2.cloned.1.call-start = ((), (), s32[]{:S(2)}) async-start(), calls=%async_computation | async-start | bytes 2359296 | tf_op jit(solution)/shard_map/all_gather | solution.py:37
  66.3 6.8 %copy-start = (bf16[297,8192]{1,0:T(8,128)(2,1)S(1)}, bf16[297,8192]{1,0:T(8,128)(2,1)}, u32[]{:S(2)}) copy-start(bf16[297,8192]{1,0:T(8,128)(2,1)} %param.7) | copy-start | bytes 14598148
  73.1 81.5 %copy-start.1 = (s32[4,32]{1,0:T(4,128)S(1)}, s32[4,32]{1,0:T(4,128)}, u32[]{:S(2)}) copy-start(s32[4,32]{1,0:T(4,128)} %param.9) | copy-start | bytes 1540
Sparse Core Ops, SparseCore 0:
  15.7 50.6 all-gather.1
where the time goes:
time: 166 us; the launch traced here: 165 us
  blocking collectives  86.7 us (52%)
  waiting for transfers between devices  50 us (30%)
  between operations  14.1 us (8%)
  matrix products  5.34 us (3%)
  local copies, waits for them, and re-layouts  5.17 us (3%)
  other arithmetic  3.88 us (2%)
    all_gather x1, waiting for transfers between devices, on_device(): portion = lax.all_gather(gathered, 'vocab', axis=1, tiled=True)  50 us
    psum x1, blocking collectives, on_device(): lax.psum((policy_scale * local_sum, policy_scale * (local_first + (local_...  40.1 us
    pmax x1, blocking collectives, on_device(): lax.pmax((local_top, local_rtop), ('vocab', 'section'))  39.2 us
    all_gather x1, blocking collectives, on_device(): gathered = lax.all_gather(hidden, 'section', axis=0, tiled=True)  7.41 us
    dot_general x1, matrix products, shard_moments(): lax.dot_general(hidden_rows, policy_head, contract_dims, preferred_elemen...  3.88 us
  transfers between devices with their start and end apart: 1, of which 1 were waited for; matrix products, arithmetic and copies ran while one was open for 0% of the time, Pallas kernels for 0%

commit v1 on v0

v1 whole, which is shorter than its diff:
```python
import functools
import itertools

import jax
import jax.numpy as jnp
from jax import lax
from jax.experimental import pallas as pl
from jax.experimental.pallas import tpu as pltpu
from jax.sharding import PartitionSpec as P

MESH = pl.DeviceIdType.MESH


def split_axis(size):
    return (size // 2, 2) if size % 2 == 0 else (size, 1)


def power_of_two(size):
    return size & (size - 1) == 0


def flip(index, step, size):
    result = index
    bit = 1
    while bit < size:
        if step & bit:
            result = result + bit - 2 * bit * ((index // bit) % 2)
        bit *= 2
    return result


def target_of(index, step, size):
    if step == 0:
        return index
    return flip(index, step, size) if power_of_two(size) else (index + step) % size


def source_of(index, step, size):
    if step == 0:
        return index
    return flip(index, step, size) if power_of_two(size) else (index + size - step) % size


def merge(parts):
    tops = [part[0:1] for part in parts]
    rtops = [part[1:2] for part in parts]
    top = functools.reduce(jnp.maximum, tops)
    rtop = functools.reduce(jnp.maximum, rtops)
    total = first = cross = chosen = rtotal = 0.0
    for part in parts:
        shift = part[0:1] - top
        scale = jnp.exp(shift)
        total = total + scale * part[2:3]
        first = first + scale * (part[3:4] + shift * part[2:3])
        cross = cross + scale * part[4:5]
        chosen = chosen + part[5:6]
        rtotal = rtotal + jnp.exp(part[1:2] - rtop) * part[6:7]
    return top, rtop, total, first, cross, chosen, rtotal


def kernel(
    sizes, hid, hp, hr, tgt, msk, out_lp, out_kl, out_tot,
    blocks, rows, wp, wr, plane, line, local_sem, send_sem, recv_sem,
):
    vocab, section = sizes
    A, B = split_axis(vocab)
    X, C = split_axis(section)
    v, s = lax.axis_index("vocab"), lax.axis_index("section")
    a, b = v // B, v % B
    x, c = s // C, s % C
    dims = (A, B, X, C)
    here = (a, b, x, c)
    piece, width = hid.shape[1], hid.shape[2]
    tokens = rows.shape[0]
    micro, span = tgt.shape
    count = wp.shape[0]

    def device(at):
        return (at[0] * B + at[1], at[2] * C + at[3])

    def slot(at):
        return (at[2] * C + at[3]) * vocab + at[0] * B + at[1]

    def to(step):
        return tuple(target_of(i, d, n) for i, d, n in zip(here, step, dims))

    def back(step):
        return tuple(source_of(i, d, n) for i, d, n in zip(here, step, dims))

    own = pltpu.make_async_copy(hid.at[0], blocks.at[slot(here)], local_sem.at[0])
    own.start()
    load_p = pltpu.make_async_copy(hp, wp, local_sem.at[1])
    load_p.start()
    load_r = pltpu.make_async_copy(hr, wr, local_sem.at[2])
    load_r.start()

    line_steps = [(d, 0, 0, 0) for d in range(1, A)]
    plane_steps = [(0,) + e for e in itertools.product(range(B), range(X), range(C)) if any(e)]
    barrier = pltpu.get_barrier_semaphore()
    for step in line_steps + plane_steps:
        pl.semaphore_signal(barrier, inc=1, device_id=device(to(step)), device_id_type=MESH)
    pl.semaphore_wait(barrier, len(line_steps) + len(plane_steps))
    own.wait()

    keys = {}
    sent = []

    def view(at, half):
        ref = blocks.at[slot(at)]
        if half is None:
            return ref
        return ref.at[:, pl.ds(half * (width // 2), width // 2)]

    def copy(key, step, at, half=None):
        i = keys.setdefault(key, len(keys))
        part = view(at, half)
        op = pltpu.make_async_remote_copy(
            src_ref=part, dst_ref=part, send_sem=send_sem.at[i], recv_sem=recv_sem.at[i],
            device_id=device(to(step)), device_id_type=MESH,
        )
        op.start()
        sent.append(op)

    def arrive(key, step, at, half=None):
        i = keys.setdefault(key, len(keys))
        part = view(at, half)
        pltpu.make_async_remote_copy(
            src_ref=part, dst_ref=part, send_sem=send_sem.at[i], recv_sem=recv_sem.at[i],
            device_id=device(to(step)), device_id_type=MESH,
        ).wait_recv()

    def to_cores(step):
        for dc in range(1, C):
            copy(("core", step, dc), (0, 0, 0, dc), back(step))

    for step in line_steps:
        copy(("line", step), step, here)

    def fan(d):
        at = back((d, 0, 0, 0))
        for dx in range(1, X):
            copy(("x", d, dx), (0, 0, dx, 0), at)
        for db in range(1, B):
            copy(("b", d, db), (0, db, 0, 0), at)
        to_cores((d, 0, 0, 0))

    def cross(d):
        for dx in range(1, X):
            at = back((d, 0, dx, 0))
            arrive(("x", d, dx), (0, 0, dx, 0), at)
            for db in range(1, B):
                copy(("xb", d, dx, db), (0, db, 0, 0), at, 0)
        for db in range(1, B):
            at = back((d, db, 0, 0))
            arrive(("b", d, db), (0, db, 0, 0), at)
            for dx in range(1, X):
                copy(("bx", d, dx, db), (0, 0, dx, 0), at, 1)
        for dx in range(1, X):
            to_cores((d, 0, dx, 0))
        for db in range(1, B):
            to_cores((d, db, 0, 0))

    def corner(d):
        for dx in range(1, X):
            for db in range(1, B):
                at = back((d, db, dx, 0))
                arrive(("xb", d, dx, db), (0, db, 0, 0), at, 0)
                arrive(("bx", d, dx, db), (0, 0, dx, 0), at, 1)
                to_cores((d, db, dx, 0))

    for d in range(A + 2):
        if d < A:
            if d:
                arrive(("line", (d, 0, 0, 0)), (d, 0, 0, 0), back((d, 0, 0, 0)))
            fan(d)
        if 1 <= d < A + 1:
            cross(d - 1)
        if d >= 2:
            corner(d - 2)
    for d in range(A):
        for db, dx in itertools.product(range(B), range(X)):
            for dc in range(1, C):
                arrive(("core", (d, db, dx, 0), dc), (0, 0, 0, dc), back((d, db, dx, dc)))

    bundle = 16 // piece if piece < 16 and 16 % piece == 0 and blocks.shape[0] % (16 // piece) == 0 else 1
    high = bundle * piece

    def pack(i, carry):
        base = pl.multiple_of(i * high, high)
        rows[pl.ds(base, high), :] = jnp.concatenate(
            [blocks[i * bundle + j] for j in range(bundle)], axis=0
        )
        return carry

    lax.fori_loop(0, blocks.shape[0] // bundle, pack, 0)
    load_p.wait()
    load_r.wait()

    wanted = jnp.concatenate([tgt[i : i + 1, :] for i in range(micro)], axis=1)
    offset = (v * section + s) * count
    tile = 128 if tokens % 128 == 0 else tokens
    dims_nt = (((1,), (1,)), ((), ()))
    index = b * (X * C) + x * C + c
    moments = []
    for n in range(tokens // tile):
        mine = rows[n * tile : (n + 1) * tile, :]
        plog = lax.dot_general(wp[...], mine, dims_nt, preferred_element_type=jnp.float32)
        rlog = lax.dot_general(wr[...], mine, dims_nt, preferred_element_type=jnp.float32)
        top = jnp.max(plog, axis=0, keepdims=True)
        shift = plog - top
        weight = jnp.exp(shift)
        total = jnp.sum(weight, axis=0, keepdims=True)
        first = jnp.sum(weight * shift, axis=0, keepdims=True)
        across = jnp.sum(weight * (plog - rlog), axis=0, keepdims=True)
        ids = offset + lax.broadcasted_iota(jnp.int32, plog.shape, 0)
        chosen = jnp.sum(
            jnp.where(ids == wanted[:, n * tile : (n + 1) * tile], plog, 0.0), axis=0, keepdims=True
        )
        rtop = jnp.max(rlog, axis=0, keepdims=True)
        rtotal = jnp.sum(jnp.exp(rlog - rtop), axis=0, keepdims=True)
        moments.append(
            jnp.concatenate([top, rtop, total, first, across, chosen, rtotal, jnp.zeros_like(top)], axis=0)
        )
    plane[index] = jnp.concatenate(moments, axis=1) if len(moments) > 1 else moments[0]

    def share(kind, step, buffer, at, start):
        i = keys.setdefault((kind, step), len(keys))
        op = pltpu.make_async_remote_copy(
            src_ref=buffer.at[at], dst_ref=buffer.at[at],
            send_sem=send_sem.at[i], recv_sem=recv_sem.at[i],
            device_id=device(to(step)), device_id_type=MESH,
        )
        if start:
            op.start()
            sent.append(op)
        else:
            op.wait_recv()

    def plane_index(at):
        return at[1] * (X * C) + at[2] * C + at[3]

    for step in plane_steps:
        share("plane", step, plane, plane_index(here), True)
    for step in plane_steps:
        share("plane", step, plane, plane_index(back(step)), False)
    merged = merge([plane[i] for i in range(B * X * C)])
    line[a] = jnp.concatenate(list(merged) + [jnp.zeros_like(merged[0])], axis=0)
    for step in line_steps:
        share("stat", step, line, a, True)
    for step in line_steps:
        share("stat", step, line, back(step)[0], False)
    top, rtop, total, first, across, chosen, rtotal = merge([line[i] for i in range(A)])
    log_total = jnp.log(total)
    lse = top + log_total
    logprob = chosen - lse
    entropy = log_total - first / total
    divergence = across / total - lse + (rtop + jnp.log(rtotal))
    mask = jnp.concatenate([msk[i : i + 1, :] for i in range(micro)], axis=1).astype(jnp.float32)
    scale = 1.0 / (micro * span)
    out_tot[0] = jnp.sum(mask * logprob) * scale
    out_tot[1] = jnp.sum(mask * entropy) * scale
    out_tot[2] = jnp.sum(mask * divergence) * scale
    for i in range(micro):
        out_lp[i : i + 1, :] = logprob[:, i * span : (i + 1) * span]
        out_kl[i : i + 1, :] = divergence[:, i * span : (i + 1) * span]
    for op in sent:
        op.wait_send()


def on_device(sizes, hidden, policy_head, reference_head, targets, loss_mask):
    vocab, section = sizes
    A, B = split_axis(vocab)
    X, C = split_axis(section)
    piece, width = hidden.shape[1], hidden.shape[2]
    devices = vocab * section
    tokens = targets.size
    copies = (
        (A - 1) + A * (X - 1 + B - 1) + 2 * A * (X - 1) * (B - 1)
        + A * B * X * (C - 1) + (B * X * C - 1) + (A - 1)
    )
    anywhere = pl.BlockSpec(memory_space=pl.ANY)
    vmem = pl.BlockSpec(memory_space=pltpu.VMEM)
    heads = policy_head.size + reference_head.size
    return pl.pallas_call(
        functools.partial(kernel, sizes),
        out_shape=(
            jax.ShapeDtypeStruct(targets.shape, jnp.float32),
            jax.ShapeDtypeStruct(targets.shape, jnp.float32),
            jax.ShapeDtypeStruct((3,), jnp.float32),
        ),
        in_specs=[anywhere, anywhere, anywhere, vmem, vmem],
        out_specs=(vmem, vmem, pl.BlockSpec(memory_space=pltpu.SMEM)),
        scratch_shapes=[
            pltpu.VMEM((devices, piece, width), hidden.dtype),
            pltpu.VMEM((tokens, width), hidden.dtype),
            pltpu.VMEM(policy_head.shape, policy_head.dtype),
            pltpu.VMEM(reference_head.shape, reference_head.dtype),
            pltpu.VMEM((B * X * C, 8, tokens), jnp.float32),
            pltpu.VMEM((A, 8, tokens), jnp.float32),
            pltpu.SemaphoreType.DMA((3,)),
            pltpu.SemaphoreType.DMA((copies,)),
            pltpu.SemaphoreType.DMA((copies,)),
        ],
        compiler_params=pltpu.CompilerParams(
            collective_id=0, has_side_effects=True, vmem_limit_bytes=60 * 1024 * 1024
        ),
        cost_estimate=pl.CostEstimate(
            flops=2 * tokens * heads, bytes_accessed=2 * heads, transcendentals=3 * tokens * policy_head.shape[0]
        ),
    )(hidden, policy_head, reference_head, targets, loss_mask)


def solution(mesh):
    placed = (
        P("section", "vocab", None),
        P(("vocab", "section"), None),
        P(("vocab", "section"), None),
        P(),
        P(),
    )
    sizes = (mesh.shape["vocab"], mesh.shape["section"])
    return jax.shard_map(
        functools.partial(on_device, sizes),
        mesh=mesh, in_specs=placed, out_specs=(P(), P(), P()), check_vma=False,
    )
```

time: 166 us -> 38.9 us (0.23)
  blocking collectives: 86.7 us -> 0 us
  waiting for transfers between devices: 50 us -> 0 us
  Pallas kernels: 0 us -> 34.3 us
  between operations: 14.1 us -> 0.64 us
  matrix products: 5.34 us -> 0 us
  other arithmetic: 3.88 us -> 0 us
    all_gather x1 -> x0, waiting for transfers between devices: 50 us -> none  [on_device(): portion = lax.all_gather(gathered, 'vocab', axis=1, tiled=True)]
    psum x1 -> x0, blocking collectives: 40.1 us -> none  [on_device(): lax.psum((policy_scale * local_sum, policy_scale * (local_first + (local_...]
    pmax x1 -> x0, blocking collectives: 39.2 us -> none  [on_device(): lax.pmax((local_top, local_rtop), ('vocab', 'section'))]
    pallas_call x0 -> x1, Pallas kernels: none -> 34.3 us  [on_device(): pl.pallas_call(functools.partial(kernel, sizes), out_shape=(jax.ShapeDtyp...]
    all_gather x1 -> x0, blocking collectives: 7.41 us -> none  [on_device(): gathered = lax.all_gather(hidden, 'section', axis=0, tiled=True)]
    dot_general x2 -> x0, matrix products: 5.34 us -> none  [the longest x1 3.88 us: shard_moments(): lax.dot_general(hidden_rows, policy_head, contract_dims, preferred_elemen...]
    all_gather x2 -> x0, local copies, waits for them, and re-layouts: 3.82 us -> none  [the longest x1 2.89 us: on_device(): portion = lax.all_gather(gathered, 'vocab', axis=1, tiled=True)]
    unnamed x4 -> x3, local copies, waits for them, and re-layouts: 0.01 us -> 3.66 us
  transfers between devices with their start and end apart: 1 -> 0, of which waited for: 1 -> 0; matrix products, arithmetic and copies ran while one was open for 0% -> 0% of each run, Pallas kernels for 0% -> 0%
where the time goes in v1:
time: 38.9 us; the launch traced here: 38.6 us
  Pallas kernels  34.3 us (88%)
  local copies, waits for them, and re-layouts  3.66 us (9%)
  between operations  0.64 us (2%)
    pallas_call x1, Pallas kernels, on_device(): pl.pallas_call(functools.partial(kernel, sizes), out_shape=(jax.ShapeDtyp...  34.3 us
    unnamed x3, local copies, waits for them, and re-layouts  3.66 us

profile of v1, /device:TPU:0, one launch (start us, length us, event | category | flops | bytes accessed | tf_op | source)
XLA Modules:
  0.0 38.6 jit_solution(2881196533684744232)
XLA Ops:
  0.6 34.3 %shard_map.76 = (f32[4,32]{1,0:T(4,128)}, f32[4,32]{1,0:T(4,128)}, f32[3]{0:T(128)}) custom-call(bf16[1,4,8192]{2,1,0:T(4,128)(2,1)} %hid.1, bf16[297,8192]{1,0:T(8,128)(2,1)} %hp.1, bf16[297,8192]{1,0:T(8,128)(2,1)} %hr.1, s32[4,32]{1,0:T(4,128)} %tgt.1, s32[4,32]{1,0:T(4,128)} %msk.1), custom_call_target="tpu_custom_call" | custom-call | flops 1245708288 | bytes 9732096 | tf_op jit(solution)/shard_map/pallas_call | solution.py:284
  35.0 1.2 %copy.11 = f32[4,32]{1,0:T(4,128)} copy(f32[4,32]{1,0:T(4,128)} %get-tuple-element.6) | data formatting | bytes 1024
  36.2 1.2 %copy.12 = f32[4,32]{1,0:T(4,128)} copy(f32[4,32]{1,0:T(4,128)} %get-tuple-element.7) | data formatting | bytes 1024
  37.4 1.2 %copy.13 = f32[3]{0:T(128)} copy(f32[3]{0:T(128)} %get-tuple-element.8) | data formatting | bytes 24
